TPU v7x, 256 devices: a whole 4x4x8 slice. The times are simulated.
256 devices in a mesh: gx: 128 (over x_lo, z, y, core), gz: 2 (over x_hi).
Axes of the slice: x: 4 (x_hi: 2, x_lo: 2; x = x_hi * 2 + x_lo), y: 4, z: 8, core: 2. Of those that a mesh axis runs over, the one named last changes fastest.
Arguments:
- cotangent: float32 [2, 4, 2048, 2048], P(None, 'gz', 'gx'), may hold values from -6 to 6
- damping: float32 [4], P('gz'), may hold values from 0.02 to 0.3
- blending: float32 [4], P('gz'), may hold values from 0.25 to 0.75
Outputs:
- grad_velocity: float32 [2, 4, 2048, 2048], P(None, 'gz', 'gx')
All inputs are finite; a program needn't handle non-finite values.
Results may differ from a plain program's by a relative error of at most 0.000096.
Values sent between devices are 32-bit elements; how exact they have to be, the bound alone decides.
A program may use at most 64 MiB of HBM per device.

v0:
```python
import functools
import math

import jax
import jax.numpy as jnp
import numpy as np
from jax import lax
from jax.experimental import pallas as pl
from jax.experimental.pallas import tpu as pltpu
from jax.sharding import PartitionSpec as P

NX = 2048
NY = 2048
CHIPS = 128
LANES = 128
GROUPS = 8
CHUNKS = 2
KEYS = 4 // CHUNKS
ROWS = 2 * KEYS
MESH = pl.DeviceIdType.MESH
F32 = jnp.float32
BF16 = jnp.bfloat16


def split_const(table):
    table = np.asarray(table, np.float32)
    high = table.astype(BF16)
    low = (table - high.astype(np.float32)).astype(BF16)
    return np.stack([high, low])


def wave(numerator, period):
    angle = 2.0 * np.pi * (np.asarray(numerator, np.int64) % period) / period
    return np.cos(angle), np.sin(angle)


@functools.cache
def tables():
    d = np.arange(128)[:, None]
    b = np.arange(128)[None, :]
    groups = []
    for c in range(1, 8):
        cos, sin = wave(b * (c + 16 * d), NY)
        groups.append(np.concatenate([cos, -sin], axis=1))
    main = split_const(np.stack(groups))
    half = np.arange(64)[:, None]
    cos0, sin0 = wave(b * (16 * half), NY)
    cos8, sin8 = wave(b * (8 + 16 * half), NY)
    im0 = -sin0
    im0[0] = 1.0 - 2.0 * (np.arange(128) % 2)
    zero = np.zeros((64, 128))
    packed = np.block([[cos0, zero, im0, zero], [zero, cos8, zero, -sin8]])
    packed = split_const(packed)
    core, x_lo, y, z = np.meshgrid(range(2), range(2), range(4), range(8), indexing="ij")
    slab = (x_lo * 64 + z * 8 + y * 2 + core).reshape(-1)
    k1 = np.arange(128)
    cos, sin = wave(k1[:, None] * slab[None, :], 128)
    slab_fwd = split_const(np.concatenate([cos, sin], axis=1))
    slab_inv = split_const(np.concatenate([cos.T, -sin.T], axis=1))
    lane = np.arange(128)
    cos, sin = wave(k1[:, None] * (lane % 16)[None, :], NX)
    sign = np.where(lane < 64, 1.0, -1.0)[None, :]
    twiddle = np.stack([cos, sin * sign]).astype(np.float32)
    src, dst = lane[:, None], lane[None, :]
    same = (src // 16) % 4 == (dst // 16) % 4
    cos, sin = wave((src % 16) * (dst % 16), 16)
    src_im, dst_im = src // 64, dst // 64
    fwd = np.where(src_im == dst_im, cos, np.where(dst_im == 0, sin, -sin)) * same
    inv = np.where(src_im == dst_im, cos, np.where(dst_im == 0, -sin, sin))
    mix = split_const(np.concatenate([fwd, fwd[:, lane ^ 32]], axis=1))
    row = np.arange(256)[:, None]
    col = np.arange(256)[None, :]
    level_row = (row // 128) * 2 + (row // 16) % 2
    level_col = (col // 128) * 2 + (col // 16) % 2
    same_c = (row // 32) % 2 == (col // 32) % 2
    inv = np.tile(inv, (2, 2)) * same_c
    keep = inv * (level_row == level_col)
    carry = inv * (level_row + 1 == level_col)
    vertical = np.stack([keep, carry]).astype(np.float32)
    return main, packed, slab_fwd, slab_inv, twiddle, mix, vertical


def split(value):
    high = value.astype(BF16)
    low = (value - high.astype(F32)).astype(BF16)
    return high, low


def dot(a, b, dims):
    return lax.dot_general(a, b, (dims, ((), ())), preferred_element_type=F32)


def dot_const_left(table, high, low, dims=((1,), (0,))):
    c_high, c_low = table
    return dot(c_high, high, dims) + (dot(c_low, high, dims) + dot(c_high, low, dims))


def dot_const_right(high, low, table, dims=((1,), (0,))):
    c_high, c_low = table
    return dot(high, c_high, dims) + (dot(low, c_high, dims) + dot(high, c_low, dims))


def kernel(
    x_ref, damp_ref, blend_ref, main_ref, packed_ref, slabf_ref, slabi_ref, twid_ref, mix_ref, vert_ref,
    out_ref,
    fold, yf, sib_f, w1, r1, coef, vmat, w2, r2, own_b, yb, acc_e, acc_o, par,
    core_f_s, core_f_r, chip_f_s, chip_f_r, chip_b_s, chip_b_r, core_b_s, core_b_r, par_s, par_r, self_sem,
):
    gx = lax.axis_index("gx")
    gz = lax.axis_index("gz")
    x_lo, z, y, core = gx // 64, (gx // 8) % 8, (gx // 2) % 4, gx % 2
    x = gz * 2 + x_lo
    me = x * 32 + y * 8 + z
    other = 1 - core
    sibling = (gx + 1 - 2 * core, gz)

    def for_chips(act):
        def step(i, carry):
            xx, yy = (x + i // 4) % 4, (y + i % 4) % 4
            for dz in range(8):
                zz = (z + dz) % 8
                act(xx * 32 + yy * 8 + zz, ((xx % 2) * 64 + zz * 8 + yy * 2 + core, xx // 2))
            return carry

        for dz in range(1, 8):
            zz = (z + dz) % 8
            act(x * 32 + y * 8 + zz, (x_lo * 64 + zz * 8 + y * 2 + core, gz))
        lax.fori_loop(1, 16, step, 0)

    barrier = pltpu.get_barrier_semaphore()

    def signal(_, device):
        pl.semaphore_signal(barrier, inc=1, device_id=device, device_id_type=MESH)

    signal(0, sibling)
    for_chips(signal)

    def piece(a):
        return x_ref[:, a * 128 : (a + 1) * 128]

    fold[0] = piece(0)
    fold[8] = piece(8)
    for a in range(1, 8):
        first, second = piece(a), piece(16 - a)
        fold[a] = first + second
        fold[8 + a] = first - second

    def y_forward(group):
        if group < 7:
            c = group + 1
            real = fold[0] + (-1.0) ** c * fold[8]
            imag = None
            for a in range(1, 8):
                real = real + math.cos(2.0 * math.pi * a * c / 16) * fold[a]
                term = -math.sin(2.0 * math.pi * a * c / 16) * fold[8 + a]
                imag = term if imag is None else imag + term
            stacked = jnp.concatenate(
                [jnp.concatenate([real, -imag], axis=1), jnp.concatenate([imag, real], axis=1)], axis=0
            )
            table = (main_ref[0, group], main_ref[1, group])
        else:
            even = fold[0] + fold[8]
            for a in (2, 4, 6):
                even = even + fold[a]
            odd = fold[1]
            for a in (3, 5, 7):
                odd = odd + fold[a]
            pair = jnp.concatenate([even + odd, even - odd], axis=1)
            zero = jnp.zeros_like(pair)
            stacked = jnp.concatenate(
                [jnp.concatenate([pair, zero], axis=1), jnp.concatenate([zero, pair], axis=1)], axis=0
            )
            table = (packed_ref[0], packed_ref[1])
        high, low = split(stacked)
        yf[group] = dot_const_left(table, high, low, ((1,), (1,)))

    def groups_of(chunk):
        return [half * 4 + chunk * KEYS + t for half in range(2) for t in range(KEYS)]

    def core_copy(src, dst, chunk, send, recv):
        return pltpu.make_async_remote_copy(
            src_ref=src, dst_ref=dst, send_sem=send.at[chunk], recv_sem=recv.at[chunk],
            device_id=sibling, device_id_type=MESH,
        )

    def forward_core(chunk):
        return core_copy(yf.at[pl.ds(other * 4 + chunk * KEYS, KEYS)], sib_f.at[chunk], chunk, core_f_s, core_f_r)

    def chip_send(src, dst, chunk, send, recv):
        def go(chip, device):
            pltpu.make_async_remote_copy(
                src_ref=src.at[chunk, pl.ds(chip * ROWS, ROWS)],
                dst_ref=dst.at[chunk, pl.ds(me * ROWS, ROWS)],
                send_sem=send.at[chunk], recv_sem=recv.at[chunk],
                device_id=device, device_id_type=MESH,
            ).start()

        mine = pl.ds(me * ROWS, ROWS)
        pltpu.make_async_copy(src.at[chunk, mine], dst.at[chunk, mine], self_sem).start()
        for_chips(go)
        pltpu.make_async_copy(src.at[chunk, mine], dst.at[chunk, mine], self_sem).wait()

    def chip_wait(ref, chunk, sem):
        most = ref.at[chunk, pl.ds(0, 127 * ROWS)]
        pltpu.make_async_copy(most, most, sem.at[chunk]).wait()

    for group in groups_of(0):
        y_forward(group)
    pl.semaphore_wait(barrier, CHIPS)
    lane = lax.broadcasted_iota(jnp.int32, (8, 128), 1)
    row8 = lax.broadcasted_iota(jnp.int32, (8, 128), 0)
    upper = (lane // 16) % 2 == 1
    par[gz] = jnp.where(
        row8 < 4,
        jnp.where(upper, damp_ref[1], damp_ref[0]),
        jnp.where(upper, blend_ref[1], blend_ref[0]),
    )
    par_copy = pltpu.make_async_remote_copy(
        src_ref=par.at[gz], dst_ref=par.at[gz], send_sem=par_s, recv_sem=par_r,
        device_id=(gx, 1 - gz), device_id_type=MESH,
    )
    par_copy.start()

    def interleave(chunk):
        for t in range(KEYS):
            w1[chunk, pl.ds(t * 2 + core, CHIPS, stride=ROWS), :] = yf[core * 4 + chunk * KEYS + t]
            w1[chunk, pl.ds(t * 2 + other, CHIPS, stride=ROWS), :] = sib_f[chunk, t]

    forward_core(0).start()
    for chunk in range(CHUNKS):
        if chunk + 1 < CHUNKS:
            for group in groups_of(chunk + 1):
                y_forward(group)
        forward_core(chunk).wait_recv()
        if chunk + 1 < CHUNKS:
            forward_core(chunk + 1).start()
        interleave(chunk)
        chip_send(w1, r1, chunk, chip_f_s, chip_f_r)

    par_copy.wait()
    lane = lax.broadcasted_iota(jnp.int32, (128, 128), 1)
    mode = lax.broadcasted_iota(jnp.int32, (128, 128), 0) + 128 * (lane % 16)
    wave_x = jnp.where(mode < NX // 2, mode, mode - NX)
    wave_x = jnp.where(mode == NX // 2, 0, wave_x)
    along_x = (2.0 * math.pi / NX) * wave_x.astype(F32)
    second = (lane // 32) % 2 == 1
    for t in range(4):
        group = core * 4 + t
        slot = jnp.where(me < 64, me * 16, 8 + (me - 64) * 16)
        number = jnp.where(group == 7, slot, group + 1 + 16 * me)
        number = jnp.where(number < NY // 2, number, number - NY)
        once = jnp.logical_and(group == 7, me == 0)
        scale = jnp.where(once, 1.0, 2.0) * (1.0 / (NX * NY))
        along_y = jnp.full((128, 128), (2.0 * math.pi / NY) * number.astype(F32))
        squared = along_x * along_x + along_y * along_y
        anchor = squared == 0.0
        inverse = jnp.where(anchor, 0.0, 1.0 / jnp.where(anchor, 1.0, squared))
        cross = jnp.where(second, along_x, along_y)
        straight = jnp.where(anchor, 1.0, cross * cross * inverse) * scale
        mixed = -along_x * along_y * inverse * scale
        for half in range(2):
            damper = jnp.exp(-par[half, 0:1, :] * squared)
            coef[t, half, 0] = straight * damper
            coef[t, half, 1] = mixed * damper
    level_row = lax.broadcasted_iota(jnp.int32, (256, 256), 0)
    level_row = level_row // 128 * 2 + (level_row // 16) % 2
    weight = jnp.zeros((256, 256), F32)
    for level in range(4):
        value = jnp.max(par[level // 2, 4:5, (level % 2) * 16 : (level % 2) * 16 + 16])
        weight = jnp.where(level_row == level, value, weight)
    high, low = split(vert_ref[0] * weight + vert_ref[1] * (1.0 - weight))
    vmat[0] = high
    vmat[1] = low

    sign = jnp.where(lane < 64, 1.0, -1.0)

    def spun(value):
        return pltpu.roll(value, 64, axis=1)

    def doubled(first, second):
        top = jnp.concatenate([first, second], axis=1)
        bottom = jnp.concatenate([spun(first) * sign, spun(second) * sign], axis=1)
        return split(jnp.concatenate([top, bottom], axis=0))

    def column(chunk, local):
        t = chunk * KEYS + local
        even = r1[chunk, pl.ds(local * 2, CHIPS, stride=ROWS), :]
        odd = r1[chunk, pl.ds(local * 2 + 1, CHIPS, stride=ROWS), :]
        halves = [jnp.concatenate([even[h * 64 : h * 64 + 64], odd[h * 64 : h * 64 + 64]], axis=0) for h in range(2)]
        high, low = doubled(*halves)
        step = dot_const_left((slabf_ref[0], slabf_ref[1]), high, low)
        turned = []
        for h in range(2):
            part = step[:, h * 128 : h * 128 + 128]
            turned.append(part * twid_ref[0] + spun(part) * twid_ref[1])
        high, low = split(jnp.concatenate(turned, axis=0))
        modes = dot_const_right(high, low, (mix_ref[0], mix_ref[1]))
        kept = []
        for h in range(2):
            rows = slice(h * 128, h * 128 + 128)
            kept.append(modes[rows, :128] * coef[t, h, 0] + modes[rows, 128:] * coef[t, h, 1])
        high, low = split(jnp.concatenate(kept, axis=1))
        back = dot_const_right(high, low, (vmat[0], vmat[1]))
        turned = []
        for h in range(2):
            part = back[:, h * 128 : h * 128 + 128]
            turned.append(part * twid_ref[0] - spun(part) * twid_ref[1])
        high, low = doubled(*turned)
        result = dot_const_left((slabi_ref[0], slabi_ref[1]), high, low)
        for h in range(2):
            for c in range(2):
                w2[chunk, pl.ds(h * 64 * ROWS + local * 2 + c, 64, stride=ROWS), :] = result[
                    c * 64 : c * 64 + 64, h * 128 : h * 128 + 128
                ]

    for chunk in range(CHUNKS):
        chip_wait(r1, chunk, chip_f_r)
        for local in range(KEYS):
            column(chunk, local)
        chip_send(w2, r2, chunk, chip_b_s, chip_b_r)

    def backward_core(chunk):
        return core_copy(own_b.at[chunk], yb.at[pl.ds(core * 4 + chunk * KEYS, KEYS)], chunk, core_b_s, core_b_r)

    def y_backward(group):
        data = yb[group].T
        high, low = split(data)
        if group < 7:
            c = group + 1
            full = dot_const_right(high, low, (main_ref[0, group], main_ref[1, group]))
            real = full[:64, :128] + full[64:, 128:]
            imag = full[64:, :128] - full[:64, 128:]
            for a in range(9):
                factor = math.cos(2.0 * math.pi * a * c / 16)
                acc_e[a] = factor * real if group == 0 else acc_e[a] + factor * real
            for a in range(1, 8):
                factor = math.sin(2.0 * math.pi * a * c / 16)
                acc_o[a] = factor * imag if group == 0 else acc_o[a] + factor * imag
        else:
            both = dot_const_right(high[:64], low[:64], (packed_ref[0, :, :256], packed_ref[1, :, :256]))
            both = both + dot_const_right(high[64:], low[64:], (packed_ref[0, :, 256:], packed_ref[1, :, 256:]))
            for a in range(9):
                acc_e[a] = acc_e[a] + (both[:, :128] + (-1.0) ** a * both[:, 128:])

    for chunk in range(CHUNKS):
        chip_wait(r2, chunk, chip_b_r)
        for t in range(KEYS):
            own_b[chunk, t] = r2[chunk, pl.ds(t * 2 + other, CHIPS, stride=ROWS), :]
        backward_core(chunk).start()
        for t in range(KEYS):
            yb[core * 4 + chunk * KEYS + t] = r2[chunk, pl.ds(t * 2 + core, CHIPS, stride=ROWS), :]
        backward_core(chunk).wait_recv()
        for group in groups_of(chunk):
            y_backward(group)

    out_ref[:, 0:128] = acc_e[0]
    out_ref[:, 1024:1152] = acc_e[8]
    for a in range(1, 8):
        out_ref[:, a * 128 : a * 128 + 128] = acc_e[a] - acc_o[a]
        out_ref[:, (16 - a) * 128 : (16 - a) * 128 + 128] = acc_e[a] + acc_o[a]

    for chunk in range(CHUNKS):
        forward_core(chunk).wait_send()
        backward_core(chunk).wait_send()
        chip_wait(w1, chunk, chip_f_s)
        chip_wait(w2, chunk, chip_b_s)


def body(cotangent, damping, blending):
    consts = [jnp.asarray(table) for table in tables()]
    vmem = pl.BlockSpec(memory_space=pltpu.VMEM)
    smem = pl.BlockSpec(memory_space=pltpu.SMEM)
    dma = pltpu.SemaphoreType.DMA
    scratch = [
        ((16, 64, 128), F32),
        ((8, 128, 128), F32),
        ((CHUNKS, KEYS, 128, 128), F32),
        ((CHUNKS, CHIPS * ROWS, 128), F32),
        ((CHUNKS, CHIPS * ROWS, 128), F32),
        ((4, 2, 2, 128, 128), F32),
        ((2, 256, 256), BF16),
        ((CHUNKS, CHIPS * ROWS, 128), F32),
        ((CHUNKS, CHIPS * ROWS, 128), F32),
        ((CHUNKS, KEYS, 128, 128), F32),
        ((8, 128, 128), F32),
        ((9, 64, 128), F32),
        ((8, 64, 128), F32),
        ((2, 8, 128), F32),
    ]
    result = pl.pallas_call(
        kernel,
        out_shape=jax.ShapeDtypeStruct((64, NY), F32),
        in_specs=[vmem, smem, smem] + [vmem] * len(consts),
        out_specs=vmem,
        scratch_shapes=[pltpu.VMEM(*s) for s in scratch] + [dma((CHUNKS,))] * 8 + [dma, dma, dma],
        compiler_params=pltpu.CompilerParams(
            collective_id=0, has_side_effects=True, vmem_limit_bytes=48 * 1024 * 1024
        ),
    )(cotangent.reshape(64, NY), damping, blending, *consts)
    return result.reshape(2, 2, 16, NY)


def solution(mesh):
    return jax.shard_map(
        body,
        mesh=mesh,
        in_specs=(P(None, "gz", "gx", None), P("gz"), P("gz")),
        out_specs=P(None, "gz", "gx", None),
        check_vma=False,
    )
```

profile of v0, /device:TPU:1, one launch (start us, length us, event | category | flops | bytes accessed | tf_op | source)
XLA Modules:
  0.0 56.1 jit_solution(17133078340356617562)
XLA Ops:
  0.0 0.0 copy-start.9
  0.0 0.0 copy-start.8
  0.0 0.7 %copy-done.9 = f32[2]{0:T(128)S(1)} copy-done((f32[2]{0:T(128)S(1)}, f32[2]{0:T(128)}, u32[]{:S(2)}) %copy-start.9) | copy-done | bytes 32
  0.7 0.0 copy-done.8
  0.7 0.0 copy-start
  0.7 1.2 %copy-done = bf16[2,7,128,256]{3,2,1,0:T(8,128)(2,1)S(1)} copy-done((bf16[2,7,128,256]{3,2,1,0:T(8,128)(2,1)S(1)}, bf16[2,7,128,256]{3,2,1,0:T(8,128)(2,1)}, u32[]{:S(2)}) %copy-start) | copy-done | bytes 917528
  1.9 0.0 copy-start.1
  1.9 1.0 %copy-done.1 = f32[2,2,16,2048]{3,2,1,0:T(8,128)S(1)} copy-done((f32[2,2,16,2048]{3,2,1,0:T(8,128)S(1)}, f32[2,2,16,2048]{3,2,1,0:T(8,128)}, u32[]{:S(2)}) %copy-start.1) | copy-done | bytes 524312
  2.9 0.0 copy-start.2
  2.9 1.0 %copy-done.2 = f32[2,256,256]{2,1,0:T(8,128)S(1)} copy-done((f32[2,256,256]{2,1,0:T(8,128)S(1)}, f32[2,256,256]{2,1,0:T(8,128)}, u32[]{:S(2)}) %copy-start.2) | copy-done | bytes 524312
  3.9 0.0 copy-start.3
  3.9 0.9 %copy-done.3 = bf16[2,128,512]{2,1,0:T(8,128)(2,1)S(1)} copy-done((bf16[2,128,512]{2,1,0:T(8,128)(2,1)S(1)}, bf16[2,128,512]{2,1,0:T(8,128)(2,1)}, u32[]{:S(2)}) %copy-start.3) | copy-done | bytes 262168
  4.9 0.0 copy-start.4
  4.9 0.9 %copy-done.4 = bf16[2,128,256]{2,1,0:T(8,128)(2,1)S(1)} copy-done((bf16[2,128,256]{2,1,0:T(8,128)(2,1)S(1)}, bf16[2,128,256]{2,1,0:T(8,128)(2,1)}, u32[]{:S(2)}) %copy-start.4) | copy-done | bytes 131096
  5.8 0.0 copy-start.5
  5.8 0.9 %copy-done.5 = f32[2,128,128]{2,1,0:T(8,128)S(1)} copy-done((f32[2,128,128]{2,1,0:T(8,128)S(1)}, f32[2,128,128]{2,1,0:T(8,128)}, u32[]{:S(2)}) %copy-start.5) | copy-done | bytes 131096
  6.7 0.0 copy-start.6
  6.7 0.9 %copy-done.6 = bf16[2,128,256]{2,1,0:T(8,128)(2,1)S(1)} copy-done((bf16[2,128,256]{2,1,0:T(8,128)(2,1)S(1)}, bf16[2,128,256]{2,1,0:T(8,128)(2,1)}, u32[]{:S(2)}) %copy-start.6) | copy-done | bytes 131096
  7.6 0.0 copy-start.7
  7.6 0.9 %copy-done.7 = bf16[2,128,256]{2,1,0:T(8,128)(2,1)S(1)} copy-done((bf16[2,128,256]{2,1,0:T(8,128)(2,1)S(1)}, bf16[2,128,256]{2,1,0:T(8,128)(2,1)}, u32[]{:S(2)}) %copy-start.7) | copy-done | bytes 131096
  8.5 46.8 %shard_map.100 = f32[64,2048]{1,0:T(8,128)S(1)} custom-call(f32[64,2048]{1,0:T(8,128)S(1)} %bitcast.3, f32[2]{0:T(128)S(1)} %copy-done.8, f32[2]{0:T(128)S(1)} %copy-done.9, bf16[2,7,128,256]{3,2,1,0:T(8,128)(2,1)S(1)} %copy-done, bf16[2,128,512]{2,1,0:T(8,128)(2,1)S(1)} %copy-done.3, bf16[2,128,256]{2,1,0:T(8,128)(2,1)S(1)} %copy-done.7, ...), custom_call_target="tpu_custom_call" | custom-call | tf_op jit(solution)/shard_map/pallas_call | solution.py:390
  55.3 0.8 %copy.12 = f32[2,2,16,2048]{3,2,1,0:T(8,128)} copy(f32[2,2,16,2048]{3,2,1,0:T(8,128)S(1)} %bitcast.2) | data formatting | bytes 1048576
Async XLA Ops:
  0.0 0.7 %copy-start.9 = (f32[2]{0:T(128)S(1)}, f32[2]{0:T(128)}, u32[]{:S(2)}) copy-start(f32[2]{0:T(128)} %blend_ref.1) | copy-start | bytes 28
  0.0 0.7 %copy-start.8 = (f32[2]{0:T(128)S(1)}, f32[2]{0:T(128)}, u32[]{:S(2)}) copy-start(f32[2]{0:T(128)} %damp_ref.1) | copy-start | bytes 28
  0.7 1.2 %copy-start = (bf16[2,7,128,256]{3,2,1,0:T(8,128)(2,1)S(1)}, bf16[2,7,128,256]{3,2,1,0:T(8,128)(2,1)}, u32[]{:S(2)}) copy-start(bf16[2,7,128,256]{3,2,1,0:T(8,128)(2,1)} %constant.14.clone.main_ref) | copy-start | bytes 2752516
  1.9 1.0 %copy-start.1 = (f32[2,2,16,2048]{3,2,1,0:T(8,128)S(1)}, f32[2,2,16,2048]{3,2,1,0:T(8,128)}, u32[]{:S(2)}) copy-start(f32[2,2,16,2048]{3,2,1,0:T(8,128)} %param.10) | copy-start | bytes 1572868
  2.9 1.0 %copy-start.2 = (f32[2,256,256]{2,1,0:T(8,128)S(1)}, f32[2,256,256]{2,1,0:T(8,128)}, u32[]{:S(2)}) copy-start(f32[2,256,256]{2,1,0:T(8,128)} %constant.20.clone.vert_ref) | copy-start | bytes 1572868
  3.9 0.9 %copy-start.3 = (bf16[2,128,512]{2,1,0:T(8,128)(2,1)S(1)}, bf16[2,128,512]{2,1,0:T(8,128)(2,1)}, u32[]{:S(2)}) copy-start(bf16[2,128,512]{2,1,0:T(8,128)(2,1)} %constant.15.clone.packed_ref) | copy-start | bytes 786436
  4.9 0.9 %copy-start.4 = (bf16[2,128,256]{2,1,0:T(8,128)(2,1)S(1)}, bf16[2,128,256]{2,1,0:T(8,128)(2,1)}, u32[]{:S(2)}) copy-start(bf16[2,128,256]{2,1,0:T(8,128)(2,1)} %constant.19.clone.mix_ref) | copy-start | bytes 393220
  5.8 0.9 %copy-start.5 = (f32[2,128,128]{2,1,0:T(8,128)S(1)}, f32[2,128,128]{2,1,0:T(8,128)}, u32[]{:S(2)}) copy-start(f32[2,128,128]{2,1,0:T(8,128)} %constant.18.clone.twid_ref) | copy-start | bytes 393220
  6.7 0.9 %copy-start.6 = (bf16[2,128,256]{2,1,0:T(8,128)(2,1)S(1)}, bf16[2,128,256]{2,1,0:T(8,128)(2,1)}, u32[]{:S(2)}) copy-start(bf16[2,128,256]{2,1,0:T(8,128)(2,1)} %constant.17.clone.slabi_ref) | copy-start | bytes 393220
  7.6 0.9 %copy-start.7 = (bf16[2,128,256]{2,1,0:T(8,128)(2,1)S(1)}, bf16[2,128,256]{2,1,0:T(8,128)(2,1)}, u32[]{:S(2)}) copy-start(bf16[2,128,256]{2,1,0:T(8,128)(2,1)} %constant.16.clone.slabf_ref) | copy-start | bytes 393220
where the time goes:
time: 56.4 us; the launch traced here: 56.1 us
  Pallas kernels  46.8 us (83%)
  local copies, waits for them, and re-layouts  9.29 us (16%)
    pallas_call x1, Pallas kernels, body(): pl.pallas_call(kernel, out_shape=jax.ShapeDtypeStruct((64, NY), F32), in_...  46.8 us
    unnamed x21, local copies, waits for them, and re-layouts  9.29 us

commit v1 on v0

--- a/solution.py
+++ b/solution.py
@@ -101,10 +101,11 @@
 
 
 def kernel(
+    x_hbm, damp_hbm, blend_hbm, main_hbm, packed_hbm, slabf_hbm, slabi_hbm, twid_hbm, mix_hbm, vert_hbm,
+    out_ref,
     x_ref, damp_ref, blend_ref, main_ref, packed_ref, slabf_ref, slabi_ref, twid_ref, mix_ref, vert_ref,
-    out_ref,
     fold, yf, sib_f, w1, r1, coef, vmat, w2, r2, own_b, yb, acc_e, acc_o, par,
-    core_f_s, core_f_r, chip_f_s, chip_f_r, chip_b_s, chip_b_r, core_b_s, core_b_r, par_s, par_r, self_sem,
+    core_f_s, core_f_r, chip_f_s, chip_f_r, chip_b_s, chip_b_r, core_b_s, core_b_r, par_s, par_r, self_sem, load_sem,
 ):
     gx = lax.axis_index("gx")
     gz = lax.axis_index("gz")
@@ -127,6 +128,11 @@
             act(x * 32 + y * 8 + zz, (x_lo * 64 + zz * 8 + y * 2 + core, gz))
         lax.fori_loop(1, 16, step, 0)
 
+    sources = [x_hbm, main_hbm, packed_hbm, damp_hbm, blend_hbm, slabf_hbm, twid_hbm, mix_hbm, vert_hbm, slabi_hbm]
+    targets = [x_ref, main_ref, packed_ref, damp_ref, blend_ref, slabf_ref, twid_ref, mix_ref, vert_ref, slabi_ref]
+    loads = [pltpu.make_async_copy(s, t, load_sem.at[i]) for i, (s, t) in enumerate(zip(sources, targets))]
+    for load in loads:
+        load.start()
     barrier = pltpu.get_barrier_semaphore()
 
     def signal(_, device):
@@ -134,6 +140,9 @@
 
     signal(0, sibling)
     for_chips(signal)
+
+    for load in loads[:3]:
+        load.wait()
 
     def piece(a):
         return x_ref[:, a * 128 : (a + 1) * 128]
@@ -207,6 +216,8 @@
     for group in groups_of(0):
         y_forward(group)
     pl.semaphore_wait(barrier, CHIPS)
+    for load in loads[3:]:
+        load.wait()
     lane = lax.broadcasted_iota(jnp.int32, (8, 128), 1)
     row8 = lax.broadcasted_iota(jnp.int32, (8, 128), 0)
     upper = (lane // 16) % 2 == 1
@@ -368,8 +379,7 @@
 
 def body(cotangent, damping, blending):
     consts = [jnp.asarray(table) for table in tables()]
-    vmem = pl.BlockSpec(memory_space=pltpu.VMEM)
-    smem = pl.BlockSpec(memory_space=pltpu.SMEM)
+    anywhere = pl.BlockSpec(memory_space=pltpu.HBM)
     dma = pltpu.SemaphoreType.DMA
     scratch = [
         ((16, 64, 128), F32),
@@ -390,11 +400,15 @@
     result = pl.pallas_call(
         kernel,
         out_shape=jax.ShapeDtypeStruct((64, NY), F32),
-        in_specs=[vmem, smem, smem] + [vmem] * len(consts),
-        out_specs=vmem,
-        scratch_shapes=[pltpu.VMEM(*s) for s in scratch] + [dma((CHUNKS,))] * 8 + [dma, dma, dma],
+        in_specs=[anywhere] * (3 + len(consts)),
+        out_specs=pl.BlockSpec(memory_space=pltpu.VMEM),
+        scratch_shapes=[pltpu.VMEM((64, NY), F32), pltpu.SMEM((2,), F32), pltpu.SMEM((2,), F32)]
+        + [pltpu.VMEM(c.shape, c.dtype) for c in consts]
+        + [pltpu.VMEM(*s) for s in scratch]
+        + [dma((CHUNKS,))] * 8
+        + [dma, dma, dma, dma((3 + len(consts),))],
         compiler_params=pltpu.CompilerParams(
-            collective_id=0, has_side_effects=True, vmem_limit_bytes=48 * 1024 * 1024
+            collective_id=0, has_side_effects=True, vmem_limit_bytes=62 * 1024 * 1024
         ),
     )(cotangent.reshape(64, NY), damping, blending, *consts)
     return result.reshape(2, 2, 16, NY)

time: 56.4 us -> 49.1 us (0.87)
  local copies, waits for them, and re-layouts: 9.29 us -> 1.87 us
    unnamed x21 -> x1, local copies, waits for them, and re-layouts: 9.29 us -> 1.87 us
where the time goes in v1:
time: 49.1 us; the launch traced here: 49 us
  Pallas kernels  47.1 us (96%)
  local copies, waits for them, and re-layouts  1.87 us (4%)
    pallas_call x1, Pallas kernels, body(): pl.pallas_call(kernel, out_shape=jax.ShapeDtypeStruct((64, NY), F32), in_...  47.1 us
    unnamed x1, local copies, waits for them, and re-layouts  1.87 us

profile of v1, /device:TPU:1, one launch (start us, length us, event | category | flops | bytes accessed | tf_op | source)
XLA Modules:
  0.0 49.0 jit_solution(9918891204443101410)
XLA Ops:
  0.0 47.1 %shard_map.100 = f32[64,2048]{1,0:T(8,128)} custom-call(f32[64,2048]{1,0:T(8,128)} %bitcast.3, f32[2]{0:T(128)} %damp_hbm.1, f32[2]{0:T(128)} %blend_hbm.1, bf16[2,7,128,256]{3,2,1,0:T(8,128)(2,1)} %constant.14.clone.main_hbm, bf16[2,128,512]{2,1,0:T(8,128)(2,1)} %constant.15.clone.packed_hbm, bf16[2,128,256]{2,1,0:T(8,128)(2,1)} %constant.16.clone.slabf_hbm, ...), custom_call_target="tpu_custom_call" | custom-call | tf_op jit(solution)/shard_map/pallas_call | solution.py:400
  47.1 1.9 %copy.12 = f32[2,2,16,2048]{3,2,1,0:T(8,128)} copy(f32[2,2,16,2048]{3,2,1,0:T(8,128)} %bitcast.2) | data formatting | bytes 1048576

commit v2 on v1

--- a/solution.py
+++ b/solution.py
@@ -14,7 +14,7 @@
 CHIPS = 128
 LANES = 128
 GROUPS = 8
-CHUNKS = 2
+CHUNKS = 4
 KEYS = 4 // CHUNKS
 ROWS = 2 * KEYS
 MESH = pl.DeviceIdType.MESH
@@ -116,17 +116,16 @@
     sibling = (gx + 1 - 2 * core, gz)
 
     def for_chips(act):
-        def step(i, carry):
-            xx, yy = (x + i // 4) % 4, (y + i % 4) % 4
-            for dz in range(8):
-                zz = (z + dz) % 8
-                act(xx * 32 + yy * 8 + zz, ((xx % 2) * 64 + zz * 8 + yy * 2 + core, xx // 2))
-            return carry
-
-        for dz in range(1, 8):
-            zz = (z + dz) % 8
-            act(x * 32 + y * 8 + zz, (x_lo * 64 + zz * 8 + y * 2 + core, gz))
-        lax.fori_loop(1, 16, step, 0)
+        xs = [(x + dx) % 4 for dx in range(4)]
+        ys = [(y + dy) % 4 for dy in range(4)]
+        zs = [(z + dz) % 8 for dz in range(8)]
+        for dx in (2, 1, 3, 0):
+            for dy in (2, 1, 3, 0):
+                base = xs[dx] * 32 + ys[dy] * 8
+                gbase = (xs[dx] % 2) * 64 + ys[dy] * 2 + core
+                for dz in (4, 3, 5, 2, 6, 1, 7, 0):
+                    if dx or dy or dz:
+                        act(base + zs[dz], (gbase + zs[dz] * 8, xs[dx] // 2))
 
     sources = [x_hbm, main_hbm, packed_hbm, damp_hbm, blend_hbm, slabf_hbm, twid_hbm, mix_hbm, vert_hbm, slabi_hbm]
     targets = [x_ref, main_ref, packed_ref, damp_ref, blend_ref, slabf_ref, twid_ref, mix_ref, vert_ref, slabi_ref]

time: 49.1 us -> 44.5 us (0.906)
  Pallas kernels: 47.1 us -> 42.5 us
    pallas_call x1, Pallas kernels: 47.1 us -> 42.5 us  [body(): pl.pallas_call(kernel, out_shape=jax.ShapeDtypeStruct((64, NY), F32), in_...]
where the time goes in v2:
time: 44.5 us; the launch traced here: 44.4 us
  Pallas kernels  42.5 us (96%)
  local copies, waits for them, and re-layouts  1.87 us (4%)
    pallas_call x1, Pallas kernels, body(): pl.pallas_call(kernel, out_shape=jax.ShapeDtypeStruct((64, NY), F32), in_...  42.5 us
    unnamed x1, local copies, waits for them, and re-layouts  1.87 us

profile of v2, /device:TPU:1, one launch (start us, length us, event | category | flops | bytes accessed | tf_op | source)
XLA Modules:
  0.0 44.4 jit_solution(9808119647788655514)
XLA Ops:
  0.0 42.5 %shard_map.100 = f32[64,2048]{1,0:T(8,128)} custom-call(f32[64,2048]{1,0:T(8,128)} %bitcast.3, f32[2]{0:T(128)} %damp_hbm.1, f32[2]{0:T(128)} %blend_hbm.1, bf16[2,7,128,256]{3,2,1,0:T(8,128)(2,1)} %constant.14.clone.main_hbm, bf16[2,128,512]{2,1,0:T(8,128)(2,1)} %constant.15.clone.packed_hbm, bf16[2,128,256]{2,1,0:T(8,128)(2,1)} %constant.16.clone.slabf_hbm, ...), custom_call_target="tpu_custom_call" | custom-call | tf_op jit(solution)/shard_map/pallas_call | solution.py:399
  42.5 1.9 %copy.12 = f32[2,2,16,2048]{3,2,1,0:T(8,128)} copy(f32[2,2,16,2048]{3,2,1,0:T(8,128)} %bitcast.2) | data formatting | bytes 1048576

commit v3 on v2

--- a/solution.py
+++ b/solution.py
@@ -15,8 +15,6 @@
 LANES = 128
 GROUPS = 8
 CHUNKS = 4
-KEYS = 4 // CHUNKS
-ROWS = 2 * KEYS
 MESH = pl.DeviceIdType.MESH
 F32 = jnp.float32
 BF16 = jnp.bfloat16
@@ -104,8 +102,8 @@
     x_hbm, damp_hbm, blend_hbm, main_hbm, packed_hbm, slabf_hbm, slabi_hbm, twid_hbm, mix_hbm, vert_hbm,
     out_ref,
     x_ref, damp_ref, blend_ref, main_ref, packed_ref, slabf_ref, slabi_ref, twid_ref, mix_ref, vert_ref,
-    fold, yf, sib_f, w1, r1, coef, vmat, w2, r2, own_b, yb, acc_e, acc_o, par,
-    core_f_s, core_f_r, chip_f_s, chip_f_r, chip_b_s, chip_b_r, core_b_s, core_b_r, par_s, par_r, self_sem, load_sem,
+    fold, yf, r1, coef, vmat, w2, yb, acc_e, acc_o, par,
+    fwd_s, fwd_r, bwd_s, bwd_r, par_s, par_r, self_f, self_b, load_sem,
 ):
     gx = lax.axis_index("gx")
     gz = lax.axis_index("gz")
@@ -113,19 +111,19 @@
     x = gz * 2 + x_lo
     me = x * 32 + y * 8 + z
     other = 1 - core
-    sibling = (gx + 1 - 2 * core, gz)
-
-    def for_chips(act):
+
+    def for_others(act):
         xs = [(x + dx) % 4 for dx in range(4)]
         ys = [(y + dy) % 4 for dy in range(4)]
         zs = [(z + dz) % 8 for dz in range(8)]
         for dx in (2, 1, 3, 0):
             for dy in (2, 1, 3, 0):
                 base = xs[dx] * 32 + ys[dy] * 8
-                gbase = (xs[dx] % 2) * 64 + ys[dy] * 2 + core
+                gbase = (xs[dx] % 2) * 64 + ys[dy] * 2
                 for dz in (4, 3, 5, 2, 6, 1, 7, 0):
-                    if dx or dy or dz:
-                        act(base + zs[dz], (gbase + zs[dz] * 8, xs[dx] // 2))
+                    for c in (core, other):
+                        if dx or dy or dz or c is other:
+                            act(base + zs[dz], c, (gbase + zs[dz] * 8 + c, xs[dx] // 2))
 
     sources = [x_hbm, main_hbm, packed_hbm, damp_hbm, blend_hbm, slabf_hbm, twid_hbm, mix_hbm, vert_hbm, slabi_hbm]
     targets = [x_ref, main_ref, packed_ref, damp_ref, blend_ref, slabf_ref, twid_ref, mix_ref, vert_ref, slabi_ref]
@@ -134,11 +132,10 @@
         load.start()
     barrier = pltpu.get_barrier_semaphore()
 
-    def signal(_, device):
+    def signal(chip, c, device):
         pl.semaphore_signal(barrier, inc=1, device_id=device, device_id_type=MESH)
 
-    signal(0, sibling)
-    for_chips(signal)
+    for_others(signal)
 
     for load in loads[:3]:
         load.wait()
@@ -182,39 +179,46 @@
         high, low = split(stacked)
         yf[group] = dot_const_left(table, high, low, ((1,), (1,)))
 
-    def groups_of(chunk):
-        return [half * 4 + chunk * KEYS + t for half in range(2) for t in range(KEYS)]
-
-    def core_copy(src, dst, chunk, send, recv):
-        return pltpu.make_async_remote_copy(
-            src_ref=src, dst_ref=dst, send_sem=send.at[chunk], recv_sem=recv.at[chunk],
-            device_id=sibling, device_id_type=MESH,
-        )
-
-    def forward_core(chunk):
-        return core_copy(yf.at[pl.ds(other * 4 + chunk * KEYS, KEYS)], sib_f.at[chunk], chunk, core_f_s, core_f_r)
-
-    def chip_send(src, dst, chunk, send, recv):
-        def go(chip, device):
+    def forward(chunk):
+        target = pl.ds(core * CHIPS + me, 1)
+
+        def go(chip, c, device):
             pltpu.make_async_remote_copy(
-                src_ref=src.at[chunk, pl.ds(chip * ROWS, ROWS)],
-                dst_ref=dst.at[chunk, pl.ds(me * ROWS, ROWS)],
-                send_sem=send.at[chunk], recv_sem=recv.at[chunk],
-                device_id=device, device_id_type=MESH,
+                src_ref=yf.at[c * 4 + chunk, pl.ds(chip, 1)], dst_ref=r1.at[chunk, target],
+                send_sem=fwd_s.at[chunk], recv_sem=fwd_r.at[chunk], device_id=device, device_id_type=MESH,
             ).start()
 
-        mine = pl.ds(me * ROWS, ROWS)
-        pltpu.make_async_copy(src.at[chunk, mine], dst.at[chunk, mine], self_sem).start()
-        for_chips(go)
-        pltpu.make_async_copy(src.at[chunk, mine], dst.at[chunk, mine], self_sem).wait()
-
-    def chip_wait(ref, chunk, sem):
-        most = ref.at[chunk, pl.ds(0, 127 * ROWS)]
+        forward_self(chunk).start()
+        for_others(go)
+
+    def forward_self(chunk):
+        own = yf.at[core * 4 + chunk, pl.ds(me, 1)]
+        return pltpu.make_async_copy(own, r1.at[chunk, pl.ds(core * CHIPS + me, 1)], self_f.at[chunk])
+
+    def backward(chunk):
+        target = pl.ds(me, 1)
+
+        def go(chip, c, device):
+            pltpu.make_async_remote_copy(
+                src_ref=w2.at[chunk, pl.ds(c * CHIPS + chip, 1)], dst_ref=yb.at[core * 4 + chunk, target],
+                send_sem=bwd_s.at[chunk], recv_sem=bwd_r.at[chunk], device_id=device, device_id_type=MESH,
+            ).start()
+
+        backward_self(chunk).start()
+        for_others(go)
+
+    def backward_self(chunk):
+        own = w2.at[chunk, pl.ds(core * CHIPS + me, 1)]
+        return pltpu.make_async_copy(own, yb.at[core * 4 + chunk, pl.ds(me, 1)], self_b.at[chunk])
+
+    def wait_others(sem, chunk):
+        most = r1.at[0, pl.ds(0, 255)]
         pltpu.make_async_copy(most, most, sem.at[chunk]).wait()
 
-    for group in groups_of(0):
-        y_forward(group)
-    pl.semaphore_wait(barrier, CHIPS)
+    y_forward(0)
+    y_forward(4)
+    pl.semaphore_wait(barrier, 255)
+    forward(0)
     for load in loads[3:]:
         load.wait()
     lane = lax.broadcasted_iota(jnp.int32, (8, 128), 1)
@@ -231,21 +235,10 @@
     )
     par_copy.start()
 
-    def interleave(chunk):
-        for t in range(KEYS):
-            w1[chunk, pl.ds(t * 2 + core, CHIPS, stride=ROWS), :] = yf[core * 4 + chunk * KEYS + t]
-            w1[chunk, pl.ds(t * 2 + other, CHIPS, stride=ROWS), :] = sib_f[chunk, t]
-
-    forward_core(0).start()
-    for chunk in range(CHUNKS):
-        if chunk + 1 < CHUNKS:
-            for group in groups_of(chunk + 1):
-                y_forward(group)
-        forward_core(chunk).wait_recv()
-        if chunk + 1 < CHUNKS:
-            forward_core(chunk + 1).start()
-        interleave(chunk)
-        chip_send(w1, r1, chunk, chip_f_s, chip_f_r)
+    for chunk in range(1, CHUNKS):
+        y_forward(chunk)
+        y_forward(chunk + 4)
+        forward(chunk)
 
     par_copy.wait()
     lane = lax.broadcasted_iota(jnp.int32, (128, 128), 1)
@@ -292,11 +285,11 @@
         bottom = jnp.concatenate([spun(first) * sign, spun(second) * sign], axis=1)
         return split(jnp.concatenate([top, bottom], axis=0))
 
-    def column(chunk, local):
-        t = chunk * KEYS + local
-        even = r1[chunk, pl.ds(local * 2, CHIPS, stride=ROWS), :]
-        odd = r1[chunk, pl.ds(local * 2 + 1, CHIPS, stride=ROWS), :]
-        halves = [jnp.concatenate([even[h * 64 : h * 64 + 64], odd[h * 64 : h * 64 + 64]], axis=0) for h in range(2)]
+    def column(t):
+        halves = [
+            jnp.concatenate([r1[t, h * 64 : h * 64 + 64], r1[t, CHIPS + h * 64 : CHIPS + h * 64 + 64]], axis=0)
+            for h in range(2)
+        ]
         high, low = doubled(*halves)
         step = dot_const_left((slabf_ref[0], slabf_ref[1]), high, low)
         turned = []
@@ -319,18 +312,13 @@
         result = dot_const_left((slabi_ref[0], slabi_ref[1]), high, low)
         for h in range(2):
             for c in range(2):
-                w2[chunk, pl.ds(h * 64 * ROWS + local * 2 + c, 64, stride=ROWS), :] = result[
-                    c * 64 : c * 64 + 64, h * 128 : h * 128 + 128
-                ]
+                w2[t, c * CHIPS + h * 64 : c * CHIPS + h * 64 + 64] = result[c * 64 : c * 64 + 64, h * 128 : h * 128 + 128]
 
     for chunk in range(CHUNKS):
-        chip_wait(r1, chunk, chip_f_r)
-        for local in range(KEYS):
-            column(chunk, local)
-        chip_send(w2, r2, chunk, chip_b_s, chip_b_r)
-
-    def backward_core(chunk):
-        return core_copy(own_b.at[chunk], yb.at[pl.ds(core * 4 + chunk * KEYS, KEYS)], chunk, core_b_s, core_b_r)
+        wait_others(fwd_r, chunk)
+        forward_self(chunk).wait()
+        column(chunk)
+        backward(chunk)
 
     def y_backward(group):
         data = yb[group].T
@@ -353,15 +341,10 @@
                 acc_e[a] = acc_e[a] + (both[:, :128] + (-1.0) ** a * both[:, 128:])
 
     for chunk in range(CHUNKS):
-        chip_wait(r2, chunk, chip_b_r)
-        for t in range(KEYS):
-            own_b[chunk, t] = r2[chunk, pl.ds(t * 2 + other, CHIPS, stride=ROWS), :]
-        backward_core(chunk).start()
-        for t in range(KEYS):
-            yb[core * 4 + chunk * KEYS + t] = r2[chunk, pl.ds(t * 2 + core, CHIPS, stride=ROWS), :]
-        backward_core(chunk).wait_recv()
-        for group in groups_of(chunk):
-            y_backward(group)
+        wait_others(bwd_r, chunk)
+        backward_self(chunk).wait()
+        y_backward(chunk)
+        y_backward(chunk + 4)
 
     out_ref[:, 0:128] = acc_e[0]
     out_ref[:, 1024:1152] = acc_e[8]
@@ -370,10 +353,8 @@
         out_ref[:, (16 - a) * 128 : (16 - a) * 128 + 128] = acc_e[a] + acc_o[a]
 
     for chunk in range(CHUNKS):
-        forward_core(chunk).wait_send()
-        backward_core(chunk).wait_send()
-        chip_wait(w1, chunk, chip_f_s)
-        chip_wait(w2, chunk, chip_b_s)
+        wait_others(fwd_s, chunk)
+        wait_others(bwd_s, chunk)
 
 
 def body(cotangent, damping, blending):
@@ -383,14 +364,10 @@
     scratch = [
         ((16, 64, 128), F32),
         ((8, 128, 128), F32),
-        ((CHUNKS, KEYS, 128, 128), F32),
-        ((CHUNKS, CHIPS * ROWS, 128), F32),
-        ((CHUNKS, CHIPS * ROWS, 128), F32),
+        ((CHUNKS, 2 * CHIPS, 128), F32),
         ((4, 2, 2, 128, 128), F32),
         ((2, 256, 256), BF16),
-        ((CHUNKS, CHIPS * ROWS, 128), F32),
-        ((CHUNKS, CHIPS * ROWS, 128), F32),
-        ((CHUNKS, KEYS, 128, 128), F32),
+        ((CHUNKS, 2 * CHIPS, 128), F32),
         ((8, 128, 128), F32),
         ((9, 64, 128), F32),
         ((8, 64, 128), F32),
@@ -404,8 +381,8 @@
         scratch_shapes=[pltpu.VMEM((64, NY), F32), pltpu.SMEM((2,), F32), pltpu.SMEM((2,), F32)]
         + [pltpu.VMEM(c.shape, c.dtype) for c in consts]
         + [pltpu.VMEM(*s) for s in scratch]
-        + [dma((CHUNKS,))] * 8
-        + [dma, dma, dma, dma((3 + len(consts),))],
+        + [dma((CHUNKS,))] * 4
+        + [dma, dma, dma((CHUNKS,)), dma((CHUNKS,)), dma((3 + len(consts),))],
         compiler_params=pltpu.CompilerParams(
             collective_id=0, has_side_effects=True, vmem_limit_bytes=62 * 1024 * 1024
         ),

time: 44.5 us -> 43.4 us (0.975)
  Pallas kernels: 42.5 us -> 41.4 us
    pallas_call x1, Pallas kernels: 42.5 us -> 41.4 us  [body(): pl.pallas_call(kernel, out_shape=jax.ShapeDtypeStruct((64, NY), F32), in_...]
where the time goes in v3:
time: 43.4 us; the launch traced here: 43.3 us
  Pallas kernels  41.4 us (95%)
  local copies, waits for them, and re-layouts  1.87 us (4%)
    pallas_call x1, Pallas kernels, body(): pl.pallas_call(kernel, out_shape=jax.ShapeDtypeStruct((64, NY), F32), in_...  41.4 us
    unnamed x1, local copies, waits for them, and re-layouts  1.87 us

profile of v3, /device:TPU:1, one launch (start us, length us, event | category | flops | bytes accessed | tf_op | source)
XLA Modules:
  0.0 43.3 jit_solution(4527247777531181506)
XLA Ops:
  0.0 41.4 %shard_map.100 = f32[64,2048]{1,0:T(8,128)} custom-call(f32[64,2048]{1,0:T(8,128)} %bitcast.3, f32[2]{0:T(128)} %damp_hbm.1, f32[2]{0:T(128)} %blend_hbm.1, bf16[2,7,128,256]{3,2,1,0:T(8,128)(2,1)} %constant.14.clone.main_hbm, bf16[2,128,512]{2,1,0:T(8,128)(2,1)} %constant.15.clone.packed_hbm, bf16[2,128,256]{2,1,0:T(8,128)(2,1)} %constant.16.clone.slabf_hbm, ...), custom_call_target="tpu_custom_call" | custom-call | tf_op jit(solution)/shard_map/pallas_call | solution.py:376
  41.4 1.9 %copy.12 = f32[2,2,16,2048]{3,2,1,0:T(8,128)} copy(f32[2,2,16,2048]{3,2,1,0:T(8,128)} %bitcast.2) | data formatting | bytes 1048576

commit v4 on v3

--- a/solution.py
+++ b/solution.py
@@ -103,7 +103,7 @@
     out_ref,
     x_ref, damp_ref, blend_ref, main_ref, packed_ref, slabf_ref, slabi_ref, twid_ref, mix_ref, vert_ref,
     fold, yf, r1, coef, vmat, w2, yb, acc_e, acc_o, par,
-    fwd_s, fwd_r, bwd_s, bwd_r, par_s, par_r, self_f, self_b, load_sem,
+    fwd_s, fwd_r, bwd_s, bwd_r, par_s, par_r, self_f, self_b, load_sem, pair_sem,
 ):
     gx = lax.axis_index("gx")
     gz = lax.axis_index("gz")
@@ -112,7 +112,8 @@
     me = x * 32 + y * 8 + z
     other = 1 - core
 
-    def for_others(act):
+    def for_others(act, cores=None):
+        cores = (core, other) if cores is None else cores
         xs = [(x + dx) % 4 for dx in range(4)]
         ys = [(y + dy) % 4 for dy in range(4)]
         zs = [(z + dz) % 8 for dz in range(8)]
@@ -121,7 +122,7 @@
                 base = xs[dx] * 32 + ys[dy] * 8
                 gbase = (xs[dx] % 2) * 64 + ys[dy] * 2
                 for dz in (4, 3, 5, 2, 6, 1, 7, 0):
-                    for c in (core, other):
+                    for c in cores:
                         if dx or dy or dz or c is other:
                             act(base + zs[dz], c, (gbase + zs[dz] * 8 + c, xs[dx] // 2))
 
@@ -135,7 +136,9 @@
     def signal(chip, c, device):
         pl.semaphore_signal(barrier, inc=1, device_id=device, device_id_type=MESH)
 
-    for_others(signal)
+    for_others(signal, (core,))
+    sibling = (gx + 1 - 2 * core, gz)
+    signal(me, other, sibling)
 
     for load in loads[:3]:
         load.wait()
@@ -179,7 +182,7 @@
         high, low = split(stacked)
         yf[group] = dot_const_left(table, high, low, ((1,), (1,)))
 
-    def forward(chunk):
+    def forward(chunk, apart=False):
         target = pl.ds(core * CHIPS + me, 1)
 
         def go(chip, c, device):
@@ -189,7 +192,12 @@
             ).start()
 
         forward_self(chunk).start()
-        for_others(go)
+        if apart:
+            for_others(go, (core,))
+            pl.semaphore_wait(pair_sem, 1)
+            for_others(go, (other,))
+        else:
+            for_others(go)
 
     def forward_self(chunk):
         own = yf.at[core * 4 + chunk, pl.ds(me, 1)]
@@ -217,8 +225,9 @@
 
     y_forward(0)
     y_forward(4)
-    pl.semaphore_wait(barrier, 255)
-    forward(0)
+    pl.semaphore_wait(barrier, 128)
+    pl.semaphore_signal(pair_sem, inc=1, device_id=sibling, device_id_type=MESH)
+    forward(0, True)
     for load in loads[3:]:
         load.wait()
     lane = lax.broadcasted_iota(jnp.int32, (8, 128), 1)
@@ -382,7 +391,7 @@
         + [pltpu.VMEM(c.shape, c.dtype) for c in consts]
         + [pltpu.VMEM(*s) for s in scratch]
         + [dma((CHUNKS,))] * 4
-        + [dma, dma, dma((CHUNKS,)), dma((CHUNKS,)), dma((3 + len(consts),))],
+        + [dma, dma, dma((CHUNKS,)), dma((CHUNKS,)), dma((3 + len(consts),)), pltpu.SemaphoreType.REGULAR],
         compiler_params=pltpu.CompilerParams(
             collective_id=0, has_side_effects=True, vmem_limit_bytes=62 * 1024 * 1024
         ),

time: 43.4 us -> 42.9 us (0.988)
  Pallas kernels: 41.4 us -> 40.9 us
    pallas_call x1, Pallas kernels: 41.4 us -> 40.9 us  [body(): pl.pallas_call(kernel, out_shape=jax.ShapeDtypeStruct((64, NY), F32), in_...]
where the time goes in v4:
time: 42.9 us; the launch traced here: 42.8 us
  Pallas kernels  40.9 us (95%)
  local copies, waits for them, and re-layouts  1.87 us (4%)
    pallas_call x1, Pallas kernels, body(): pl.pallas_call(kernel, out_shape=jax.ShapeDtypeStruct((64, NY), F32), in_...  40.9 us
    unnamed x1, local copies, waits for them, and re-layouts  1.87 us

profile of v4, /device:TPU:1, one launch (start us, length us, event | category | flops | bytes accessed | tf_op | source)
XLA Modules:
  0.0 42.8 jit_solution(18065975124275534118)
XLA Ops:
  0.0 40.9 %shard_map.100 = f32[64,2048]{1,0:T(8,128)} custom-call(f32[64,2048]{1,0:T(8,128)} %bitcast.3, f32[2]{0:T(128)} %damp_hbm.1, f32[2]{0:T(128)} %blend_hbm.1, bf16[2,7,128,256]{3,2,1,0:T(8,128)(2,1)} %constant.14.clone.main_hbm, bf16[2,128,512]{2,1,0:T(8,128)(2,1)} %constant.15.clone.packed_hbm, bf16[2,128,256]{2,1,0:T(8,128)(2,1)} %constant.16.clone.slabf_hbm, ...), custom_call_target="tpu_custom_call" | custom-call | tf_op jit(solution)/shard_map/pallas_call | solution.py:385
  40.9 1.9 %copy.12 = f32[2,2,16,2048]{3,2,1,0:T(8,128)} copy(f32[2,2,16,2048]{3,2,1,0:T(8,128)} %bitcast.2) | data formatting | bytes 1048576

commit v5 on v4

--- a/solution.py
+++ b/solution.py
@@ -117,12 +117,12 @@
         xs = [(x + dx) % 4 for dx in range(4)]
         ys = [(y + dy) % 4 for dy in range(4)]
         zs = [(z + dz) % 8 for dz in range(8)]
-        for dx in (2, 1, 3, 0):
-            for dy in (2, 1, 3, 0):
-                base = xs[dx] * 32 + ys[dy] * 8
-                gbase = (xs[dx] % 2) * 64 + ys[dy] * 2
-                for dz in (4, 3, 5, 2, 6, 1, 7, 0):
-                    for c in cores:
+        for c in cores:
+            for dx in (2, 1, 3, 0):
+                for dy in (2, 1, 3, 0):
+                    base = xs[dx] * 32 + ys[dy] * 8
+                    gbase = (xs[dx] % 2) * 64 + ys[dy] * 2
+                    for dz in (4, 3, 5, 2, 6, 1, 7, 0):
                         if dx or dy or dz or c is other:
                             act(base + zs[dz], c, (gbase + zs[dz] * 8 + c, xs[dx] // 2))
 

time: 42.9 us -> 43 us (level)
  no operation moved by 1% of the time
where the time goes in v5:
time: 43 us; the launch traced here: 42.8 us
  Pallas kernels  41 us (95%)
  local copies, waits for them, and re-layouts  1.87 us (4%)
    pallas_call x1, Pallas kernels, body(): pl.pallas_call(kernel, out_shape=jax.ShapeDtypeStruct((64, NY), F32), in_...  41 us
    unnamed x1, local copies, waits for them, and re-layouts  1.87 us

profile of v5, /device:TPU:1, one launch (start us, length us, event | category | flops | bytes accessed | tf_op | source)
XLA Modules:
  0.0 42.8 jit_solution(15726759453884171529)
XLA Ops:
  0.0 41.0 %shard_map.100 = f32[64,2048]{1,0:T(8,128)} custom-call(f32[64,2048]{1,0:T(8,128)} %bitcast.3, f32[2]{0:T(128)} %damp_hbm.1, f32[2]{0:T(128)} %blend_hbm.1, bf16[2,7,128,256]{3,2,1,0:T(8,128)(2,1)} %constant.14.clone.main_hbm, bf16[2,128,512]{2,1,0:T(8,128)(2,1)} %constant.15.clone.packed_hbm, bf16[2,128,256]{2,1,0:T(8,128)(2,1)} %constant.16.clone.slabf_hbm, ...), custom_call_target="tpu_custom_call" | custom-call | tf_op jit(solution)/shard_map/pallas_call | solution.py:385
  41.0 1.9 %copy.12 = f32[2,2,16,2048]{3,2,1,0:T(8,128)} copy(f32[2,2,16,2048]{3,2,1,0:T(8,128)} %bitcast.2) | data formatting | bytes 1048576
